TPU v7x, 512 devices: a whole 4x8x8 slice. The times are simulated.
512 devices in a mesh: tm: 128 (over z_lo, x, y, core), series: 4 (over z_hi).
Axes of the slice: x: 4, y: 8, z: 8 (z_hi: 4, z_lo: 2; z = z_hi * 2 + z_lo), core: 2. Of those that a mesh axis runs over, the one named last changes fastest.
Arguments:
- time_query: bfloat16 [20, 8192, 512], P('series', 'tm'), may hold values from -160 to 160
- time_key: bfloat16 [20, 8192, 512], P('series', 'tm'), may hold values from -6 to 6
- time_value: bfloat16 [20, 8192, 512], P('series', 'tm'), may hold values from -6 to 6
- group_query: bfloat16 [20, 8192, 512], P('series', 'tm'), may hold values from -160 to 160
- group_key: bfloat16 [20, 8192, 512], P('series', 'tm'), may hold values from -6 to 6
- group_value: bfloat16 [20, 8192, 512], P('series', 'tm'), may hold values from -6 to 6
- out_time: bfloat16 [512, 768], P('series'), may hold values from -0.25 to 0.25
- out_group: bfloat16 [512, 768], P('series'), may hold values from -0.25 to 0.25
- series_group: int32 [20], replicated, may hold values from 0 to 1, as said below
- band_width: int32 [8], replicated, may hold values from 2 to 16, as said below
- cotangent: bfloat16 [20, 8192, 768], P('series', 'tm'), may hold values from -6 to 6
Outputs:
- grad_time_query: bfloat16 [20, 8192, 512], P('series', 'tm')
- grad_time_key: bfloat16 [20, 8192, 512], P('series', 'tm')
- grad_time_value: bfloat16 [20, 8192, 512], P('series', 'tm')
- grad_group_query: bfloat16 [20, 8192, 512], P('series', 'tm')
- grad_group_key: bfloat16 [20, 8192, 512], P('series', 'tm')
- grad_group_value: bfloat16 [20, 8192, 512], P('series', 'tm')
- grad_out_time: float32 [512, 768], P('series', 'tm')
- grad_out_group: float32 [512, 768], P('series', 'tm')
Inputs may be any that keep to these rules, and one draw needn't show every extreme that they name: `series_group`: series with equal numbers form one group; there are two groups, one of exactly 16 series and one of exactly 4. `band_width`: some head's band is exactly 16.
All inputs are finite; a program needn't handle non-finite values.
Results may differ from a plain program's by a relative error of at most 0.0058.
Values may be sent and summed in bfloat16 or wider, within the bound.
No kernel may reach another device: no remote copies, remote signals or barrier semaphores. Data moves between devices by JAX's collectives and lax.ppermute only.
A program may use at most 128 MiB of HBM per device.

v0:
```python
import functools

import jax
import jax.numpy as jnp
import numpy as np
from jax import lax
from jax.experimental import pallas as pl
from jax.experimental.pallas import tpu as pltpu
from jax.sharding import PartitionSpec as P

HEAD_DIM = 64
BAND = 16
QUAD = 4
X_SIZE, Y_SIZE, LOW_SIZE = 4, 8, 2
MASKED = -1e30
F32 = jnp.float32
BF16 = jnp.bfloat16
NT = (((1,), (1,)), ((), ()))
NN = (((1,), (0,)), ((), ()))
TN = (((0,), (0,)), ((), ()))


def dot(left, right, dims):
    return lax.dot_general(left, right, dims, preferred_element_type=F32)


def block(operand, where):
    if where == "smem":
        return pl.BlockSpec(memory_space=pltpu.SMEM)
    if where == "any":
        return pl.BlockSpec(memory_space=pl.ANY)
    zeros = (0,) * len(operand.shape)
    return pl.BlockSpec(operand.shape, lambda i: zeros)


def call(body, out_shape, operands, flops, size, smem=(), anywhere=False, scratch=(), room=60 * 1024):
    usual = "any" if anywhere else "vmem"
    many = isinstance(out_shape, (tuple, list))
    outs = [block(o, usual) for o in out_shape] if many else block(out_shape, usual)
    return pl.pallas_call(
        body,
        out_shape=out_shape,
        grid=(1,),
        in_specs=[block(o, "smem" if n in smem else usual) for n, o in enumerate(operands)],
        out_specs=outs,
        scratch_shapes=list(scratch),
        compiler_params=pltpu.CompilerParams(vmem_limit_bytes=room * 1024),
        cost_estimate=pl.CostEstimate(flops=flops, bytes_accessed=size, transcendentals=0),
    )(*operands)


def shape(dims, dtype):
    return jax.ShapeDtypeStruct(dims, dtype)


def stacked(rows):
    lane = lax.broadcasted_iota(jnp.int32, rows.shape, 1) // HEAD_DIM
    zero = jnp.zeros_like(rows)
    return jnp.concatenate([jnp.where(lane == h, rows, zero) for h in range(QUAD)], axis=0)


def unstacked(rows):
    count = rows.shape[0] // QUAD
    low = lax.broadcasted_iota(jnp.int32, (count, 2 * HEAD_DIM), 1) < HEAD_DIM
    parts = []
    for pair in range(QUAD // 2):
        lanes = slice(2 * HEAD_DIM * pair, 2 * HEAD_DIM * (pair + 1))
        first = rows[2 * pair * count : (2 * pair + 1) * count, lanes]
        second = rows[(2 * pair + 1) * count : (2 * pair + 2) * count, lanes]
        parts.append(jnp.where(low, first, second))
    return jnp.concatenate(parts, axis=1)


def column_softmax(scores, keep):
    scores = jnp.where(keep, scores * HEAD_DIM ** (-0.5), MASKED)
    weights = jnp.exp(scores - jnp.max(scores, axis=0, keepdims=True))
    return weights * (1.0 / jnp.sum(weights, axis=0, keepdims=True))


def backward(prob, query_stack, key, value, grad_stack):
    grad_prob = dot(value, grad_stack, NT).astype(BF16).astype(F32)
    centred = grad_prob - jnp.sum(grad_prob * prob, axis=0, keepdims=True)
    grad_score = prob * centred * HEAD_DIM ** (-0.5)
    high = grad_score.astype(BF16)
    low = (grad_score - high.astype(F32)).astype(BF16)
    grad_query = dot(high, key, TN) + dot(low, key, TN)
    grad_key = dot(high, query_stack, NN) + dot(low, query_stack, NN)
    grad_value = dot(prob.astype(BF16), grad_stack, NN)
    return grad_query, grad_key, grad_value


def term_of(spread_ref, cot, mixed, scale):
    rows = dot(spread_ref[...], cot, NT).astype(BF16)
    return (dot(rows, mixed, NN) * scale).astype(BF16)


def x_of(place_ref):
    return lax.rem(place_ref[1] // (2 * Y_SIZE), X_SIZE)


def core_of(place_ref):
    return lax.rem(place_ref[1], 2)


def run_copies(copies):
    for copy in copies:
        copy.start()
    for copy in copies:
        copy.wait()


def pack_body(q_ref, k_ref, v_ref, c_ref, out_ref):
    start = 0
    for ref in (q_ref, k_ref, v_ref, c_ref):
        width = ref.shape[2]
        for target in range(out_ref.shape[0]):
            out_ref[target, :, :, start : start + width] = ref[:, 16 * target : 16 * (target + 1)]
        start += width


def piece_body(place_ref, wt_ref, wg_ref, out_ref):
    rows = out_ref.shape[1]
    spot = pl.ds(pl.multiple_of(rows * x_of(place_ref), rows), rows)
    piece = jnp.where(core_of(place_ref) == 0, wt_ref[spot], wg_ref[spot])
    for j in range(out_ref.shape[0]):
        out_ref[j] = piece


def gather_body(place_ref, *rest):
    blocks, out_ref, sems = rest[:-2], rest[-2], rest[-1]
    count = len(blocks)
    copies = []
    for shift, ref in enumerate(blocks):
        source = lax.rem(x_of(place_ref) + count - shift, count)
        copies.append(pltpu.make_async_copy(ref, out_ref.at[source], sems.at[shift]))
    run_copies(copies)


def unpack_body(place_ref, *rest):
    blocks, outs, sems = rest[:-4], rest[-4:-1], rest[-1]
    count = len(blocks)
    copies = []
    for shift, ref in enumerate(blocks):
        source = lax.rem(place_ref[0] + shift, count)
        for index, out_ref in enumerate(outs):
            width = out_ref.shape[2]
            copies.append(
                pltpu.make_async_copy(
                    ref.at[:, :, pl.ds(width * index, width)],
                    out_ref.at[:, pl.ds(pl.multiple_of(16 * source, 16), 16), :],
                    sems.at[len(copies)],
                )
            )
    run_copies(copies)


def time_forward_body(
    scale, place_ref, band_ref, q_ref, k_ref, v_ref, rim_ref, c_ref, spread_ref, prob_ref, term_ref, mixed
):
    ser, rows, width = q_ref.shape
    keys = rows + BAND
    lanes = QUAD * HEAD_DIM
    key_pos = lax.broadcasted_iota(jnp.int32, (keys, QUAD * rows), 0)
    column = lax.broadcasted_iota(jnp.int32, (keys, QUAD * rows), 1)
    offset = lax.rem(column, rows) + BAND - key_pos
    head = column // rows
    inside = key_pos >= jnp.where(place_ref[1] == 0, BAND, 0)
    for quad in range(width // lanes):
        band = jnp.where(
            head < 2,
            jnp.where(head == 0, band_ref[QUAD * quad], band_ref[QUAD * quad + 1]),
            jnp.where(head == 2, band_ref[QUAD * quad + 2], band_ref[QUAD * quad + 3]),
        )
        keep = (offset >= 0) & (offset < band) & inside
        cut = slice(lanes * quad, lanes * (quad + 1))
        for s in range(ser):
            key = jnp.concatenate([rim_ref[0, s, :, cut], k_ref[s, :, cut]], axis=0)
            value = jnp.concatenate([rim_ref[1, s, :, cut], v_ref[s, :, cut]], axis=0)
            prob = column_softmax(dot(key, stacked(q_ref[s, :, cut]), NT), keep)
            prob_ref[s, quad] = prob
            out = unstacked(dot(prob.astype(BF16), value, TN))
            mixed[rows * s : rows * (s + 1), cut] = out.astype(BF16)
    cot = c_ref[...].reshape(ser * rows, c_ref.shape[2])
    term_ref[...] = term_of(spread_ref, cot, mixed[...], scale)


def back_project(cot, own, mine_ref, other_ref, weights, grad):
    xs, parts, rows, _ = mine_ref.shape
    for x in range(xs):
        for j in range(parts):
            start = rows * (xs * j + x)
            weights[start : start + rows] = jnp.where(own, mine_ref[x, j], other_ref[x, j])
    grad[...] = dot(cot, weights[...], NT).astype(BF16)


def time_backward_body(
    place_ref, prob_ref, q_ref, k_ref, v_ref, rim_ref, c_ref, mine_ref, other_ref,
    gq_ref, gk_ref, gv_ref, tail_ref, rimg_ref, grad, weights
):
    ser, rows, width = q_ref.shape
    lanes = QUAD * HEAD_DIM
    cot = c_ref[...].reshape(ser * rows, c_ref.shape[2])
    back_project(cot, core_of(place_ref) == 0, mine_ref, other_ref, weights, grad)
    for quad in range(width // lanes):
        cut = slice(lanes * quad, lanes * (quad + 1))
        for s in range(ser):
            key = jnp.concatenate([rim_ref[0, s, :, cut], k_ref[s, :, cut]], axis=0)
            value = jnp.concatenate([rim_ref[1, s, :, cut], v_ref[s, :, cut]], axis=0)
            gq, gk, gv = backward(
                prob_ref[s, quad],
                stacked(q_ref[s, :, cut]),
                key,
                value,
                stacked(grad[rows * s : rows * (s + 1), cut]),
            )
            gq_ref[s, :, cut] = unstacked(gq).astype(BF16)
            for index, (result, ref) in enumerate(((gk, gk_ref), (gv, gv_ref))):
                rimg_ref[index, s, :, cut] = result[:BAND].astype(BF16)
                ref[s, :, cut] = result[BAND:].astype(BF16)
                tail_ref[index, s, :, cut] = result[rows:]


def time_join_body(gk_any, gv_any, tail_ref, got_ref, gk_ref, gv_ref):
    for index, ref in enumerate((gk_ref, gv_ref)):
        ref[...] = (tail_ref[index] + got_ref[index].astype(F32)).astype(BF16)


def group_ids(group_ref, series, patch, count, half):
    ids = jnp.zeros_like(series)
    for s in range(count):
        ids = jnp.where(series == s, group_ref[s], ids)
    return ids * half + patch


def half_rows(cube, part):
    half = cube.shape[1] // 2
    cube = cube.astype(F32)[:, half * part : half * (part + 1)]
    return cube.reshape(-1, cube.shape[2]).astype(BF16)


def moved_rows(x_ref, lane, part):
    parts, ser, patches, _ = x_ref.shape
    lanes = QUAD * HEAD_DIM
    cube = x_ref[:, :, :, lane : lane + lanes].reshape(parts * ser, patches, lanes)
    return half_rows(cube, part)


def group_forward_body(
    scale, group_ref, x_ref, spread_ref, time_term_ref, prob_ref, term_ref, mixed, res
):
    parts, ser, patches, _ = x_ref.shape
    series = parts * ser
    width = mixed.shape[1]
    lanes = QUAD * HEAD_DIM
    half = patches // 2
    count = series * half
    row = lax.broadcasted_iota(jnp.int32, (count, 1), 0)
    column = lax.rem(lax.broadcasted_iota(jnp.int32, (1, QUAD * count), 1), count)
    id_key = group_ids(group_ref, row // half, lax.rem(row, half), series, half)
    id_query = group_ids(group_ref, column // half, lax.rem(column, half), series, half)
    keep = id_key == id_query
    for quad in range(width // lanes):
        start = lanes * quad
        for part in range(2):
            query = stacked(moved_rows(x_ref, start, part))
            key = moved_rows(x_ref, width + start, part)
            value = moved_rows(x_ref, 2 * width + start, part)
            prob = column_softmax(dot(key, query, NT), keep)
            prob_ref[quad, part] = prob
            out = unstacked(dot(prob.astype(BF16), value, TN))
            res[:, half * part : half * (part + 1), start : start + lanes] = out.reshape(
                series, half, lanes
            )
    mixed[...] = res[...].reshape(series * patches, width).astype(BF16)
    cot = x_ref[:, :, :, 3 * width :].reshape(series * patches, spread_ref.shape[1])
    term_ref[:, :width] = time_term_ref[...]
    term_ref[:, width:] = term_of(spread_ref, cot, mixed[...], scale)


def group_backward_body(place_ref, x_ref, prob_ref, mine_ref, other_ref, *rest):
    outs, (grad, weights, res) = rest[:-3], rest[-3:]
    parts, ser, patches, _ = x_ref.shape
    series = parts * ser
    width = grad.shape[1]
    lanes = QUAD * HEAD_DIM
    half = patches // 2
    cot = x_ref[:, :, :, 3 * width :].reshape(series * patches, weights.shape[1])
    back_project(cot, core_of(place_ref) == 1, mine_ref, other_ref, weights, grad)
    for quad in range(width // lanes):
        start = lanes * quad
        for part in range(2):
            query = stacked(moved_rows(x_ref, start, part))
            key = moved_rows(x_ref, width + start, part)
            value = moved_rows(x_ref, 2 * width + start, part)
            own_grad = grad[:, start : start + lanes].reshape(series, patches, lanes)
            grad_stack = stacked(half_rows(own_grad, part))
            gq, gk, gv = backward(prob_ref[quad, part], query, key, value, grad_stack)
            for index, result in enumerate((unstacked(gq), gk, gv)):
                spot = slice(width * index + start, width * index + start + lanes)
                res[:, half * part : half * (part + 1), spot] = result.reshape(series, half, lanes)
    for shift, out_ref in enumerate(outs):
        source = lax.rem(place_ref[0] + parts - shift, parts)
        out_ref[...] = res[pl.ds(ser * source, ser)].astype(BF16)


def first_sum_body(pad_ref, in_ref, out_ref):
    total = jnp.sum(in_ref[...].astype(F32), axis=0).astype(BF16)
    total = dot(pad_ref[...], total, NN)
    lows = total.shape[0] // 8
    width = total.shape[1] // 2
    for j in range(width // 128):
        chunks = [
            total[:, start : start + 128].reshape(lows, 8, 128)
            for start in (128 * j, width + 128 * j)
        ]
        out_ref[lows * j : lows * (j + 1)] = jnp.concatenate(chunks, axis=1).astype(BF16)


def last_sum_body(in_ref, time_ref, group_ref):
    total = jnp.sum(in_ref[...].astype(F32), axis=0)
    columns = time_ref.shape[0]
    time_ref[...] = total[:columns]
    group_ref[...] = total[8 : 8 + columns]


def tm_index(low, x, y, core):
    return ((low * X_SIZE + x) * Y_SIZE + y) * 2 + core


def first_groups():
    return [
        [tm_index(low, x, y, core) for x in range(X_SIZE) for core in range(2)]
        for low in range(LOW_SIZE)
        for y in range(Y_SIZE)
    ]


def along_x(shift):
    return [
        (tm_index(low, x, y, core), tm_index(low, (x + shift) % X_SIZE, y, core))
        for low in range(LOW_SIZE)
        for x in range(X_SIZE)
        for y in range(Y_SIZE)
        for core in range(2)
    ]


def second_groups(parts, count):
    return [
        [
            j * count + tm_index(low, x, y, core)
            for j in range(parts)
            for y in range(Y_SIZE)
            for low in range(LOW_SIZE)
        ]
        for x in range(X_SIZE)
        for core in range(2)
    ]


def spread_matrix(model, count):
    columns = model // count
    order = [
        columns * tm_index(low, x, y, core) + e
        for x in range(X_SIZE)
        for core in range(2)
        for y in range(Y_SIZE)
        for low in range(LOW_SIZE)
        for e in range(columns)
    ]
    return jnp.asarray(np.eye(model, dtype=np.float32)[order], BF16)


def pad_matrix(columns):
    lows = Y_SIZE * LOW_SIZE
    pad = np.zeros((lows, 8, lows, columns), np.float32)
    for low in range(lows):
        for e in range(columns):
            pad[low, e, low, e] = 1
    return jnp.asarray(pad.reshape(8 * lows, columns * lows), BF16)


def per_device(
    time_query,
    time_key,
    time_value,
    group_query,
    group_key,
    group_value,
    out_time,
    out_group,
    series_group,
    band_width,
    cotangent,
):
    ser, rows, width = time_query.shape
    model = cotangent.shape[2]
    parts = lax.axis_size("series")
    count = lax.axis_size("tm")
    columns = model // count
    scale = float(ser * parts * rows * count) ** (-0.5)
    place = lax.axis_index("tm")
    patches = rows // parts

    series = lax.axis_index("series")
    where = jnp.stack([series, place]).astype(jnp.int32)

    def over_series(value, shift):
        return lax.ppermute(value, "series", [(j, (j + shift) % parts) for j in range(parts)])

    sem = pltpu.SemaphoreType.DMA
    piece_rows = out_time.shape[0] // X_SIZE
    piece = call(
        piece_body,
        shape((parts, piece_rows, model), BF16),
        (where, out_time, out_group),
        0,
        500_000,
        smem=(0,),
    )
    column_piece = lax.all_to_all(piece, "series", 0, 0, tiled=True)
    rim = jnp.stack([time_key[:, rows - BAND :], time_value[:, rows - BAND :]])
    rim = lax.ppermute(rim, "tm", [(i, i + 1) for i in range(count - 1)])
    packed = call(
        pack_body,
        shape((parts, ser, patches, 3 * width + model), BF16),
        (group_query, group_key, group_value, cotangent),
        0,
        3_000_000,
    )
    packed, column_piece, rim = lax.optimization_barrier((packed, column_piece, rim))
    moved = lax.all_to_all(packed, "series", 0, 0, tiled=True)
    spread = spread_matrix(model, count)
    quads = width // (QUAD * HEAD_DIM)
    prob, term_time = call(
        functools.partial(time_forward_body, scale),
        (
            shape((ser, quads, rows + BAND, QUAD * rows), F32),
            shape((model, width), BF16),
        ),
        (where, band_width, time_query, time_key, time_value, rim, cotangent, spread),
        2_000_000_000,
        6_000_000,
        smem=(0, 1),
        scratch=[pltpu.VMEM((ser * rows, width), BF16)],
    )
    pieces = [column_piece] + [
        lax.ppermute(column_piece, "tm", along_x(shift)) for shift in range(1, X_SIZE)
    ]
    order, term_time = lax.optimization_barrier((where, term_time))
    weight_mine = call(
        gather_body,
        shape((X_SIZE, parts, piece_rows, model), BF16),
        (order, *pieces),
        0,
        1_600_000,
        smem=(0,),
        anywhere=True,
        scratch=[sem((X_SIZE,))],
        room=8192,
    )
    weight_other = lax.ppermute(weight_mine, "tm", [(i, i ^ 1) for i in range(count)])

    grad_tq, grad_tk, grad_tv, tail, rim_grad = call(
        time_backward_body,
        (
            shape((ser, rows, width), BF16),
            shape((ser, rows, width), BF16),
            shape((ser, rows, width), BF16),
            shape((2, ser, BAND, width), F32),
            shape((2, ser, BAND, width), BF16),
        ),
        (
            where,
            prob,
            time_query,
            time_key,
            time_value,
            rim,
            cotangent,
            weight_mine,
            weight_other,
        ),
        4_000_000_000,
        6_000_000,
        smem=(0,),
        scratch=[pltpu.VMEM((ser * rows, width), BF16), pltpu.VMEM((width, model), BF16)],
    )
    rim_back = lax.ppermute(rim_grad, "tm", [(i + 1, i) for i in range(count - 1)])
    term_time, grad_tq = lax.optimization_barrier((term_time, grad_tq))
    total = parts * ser * patches
    group_prob, term = call(
        functools.partial(group_forward_body, scale),
        (
            shape((quads, 2, total // 2, QUAD * total // 2), F32),
            shape((model, 2 * width), BF16),
        ),
        (series_group, moved, spread, term_time),
        4_000_000_000,
        8_000_000,
        smem=(0,),
        scratch=[
            pltpu.VMEM((total, width), BF16),
            pltpu.VMEM((parts * ser, patches, width), F32),
        ],
    )
    first = 2 * X_SIZE
    plane = lax.all_to_all(
        term.reshape(first, model // first, 2 * width),
        "tm",
        0,
        0,
        tiled=True,
        axis_index_groups=first_groups(),
    )
    back = call(
        group_backward_body,
        (shape((ser, patches, 3 * width), BF16),) * parts,
        (where, moved, group_prob, weight_mine, weight_other),
        40_000_000_000,
        8_000_000,
        smem=(0,),
        scratch=[
            pltpu.VMEM((total, width), BF16),
            pltpu.VMEM((width, model), BF16),
            pltpu.VMEM((parts * ser, patches, 3 * width), F32),
        ],
    )
    plane, _ = lax.optimization_barrier((plane, back[0]))
    second = parts * Y_SIZE * LOW_SIZE
    chunks = call(
        first_sum_body,
        shape((second, 16, 128), BF16),
        (pad_matrix(columns), plane),
        0,
        500_000,
        room=8192,
    )
    returned = [back[0]] + [over_series(back[shift], -shift) for shift in range(1, parts)]

    chunks, tail = lax.optimization_barrier((chunks, tail))
    border = pl.BlockSpec((ser, BAND, width), lambda i: (0, rows // BAND - 1, 0))
    grad_tk, grad_tv = pl.pallas_call(
        time_join_body,
        out_shape=(shape((ser, rows, width), BF16),) * 2,
        grid=(1,),
        in_specs=[pl.BlockSpec(memory_space=pl.ANY)] * 2 + [block(tail, ""), block(rim_back, "")],
        out_specs=[border] * 2,
        input_output_aliases={0: 0, 1: 1},
        compiler_params=pltpu.CompilerParams(vmem_limit_bytes=60 * 1024 * 1024),
        cost_estimate=pl.CostEstimate(flops=40_000_000_000, bytes_accessed=1_000_000, transcendentals=0),
    )(grad_tk, grad_tv, tail, rim_back)
    order, grad_tk = lax.optimization_barrier((where, grad_tk))
    grad_gq, grad_gk, grad_gv = call(
        unpack_body,
        (shape((ser, rows, width), BF16),) * 3,
        (order, *returned),
        0,
        2_000_000,
        smem=(0,),
        anywhere=True,
        scratch=[sem((3 * parts,))],
        room=8192,
    )
    chunks = lax.all_to_all(
        chunks,
        ("series", "tm"),
        0,
        0,
        tiled=True,
        axis_index_groups=second_groups(parts, count),
    )
    grad_wt, grad_wg = call(
        last_sum_body, (shape((columns, 128), F32),) * 2, (chunks,), 0, 100_000, room=8192
    )
    return (grad_tq, grad_tk, grad_tv, grad_gq, grad_gk, grad_gv, grad_wt.T, grad_wg.T)


def solution(mesh):
    rows = P("series", "tm", None)
    return jax.shard_map(
        per_device,
        mesh=mesh,
        in_specs=(rows,) * 6 + (P("series", None),) * 2 + (P(), P(), rows),
        out_specs=(rows,) * 6 + (P("series", "tm"),) * 2,
        check_vma=False,
    )
```

profile of v0, /device:TPU:1, one launch (start us, length us, event | category | flops | bytes accessed | tf_op | source)
XLA Modules:
  0.0 125.1 jit_solution(17118474831996874352)
XLA Ops:
  0.6 0.6 pad_add_fusion.place_ref
  1.2 1.7 %shard_map.189 = bf16[4,32,768]{2,1,0:T(8,128)(2,1)} custom-call(s32[2]{0:T(128)} %pad_add_fusion.place_ref, bf16[128,768]{1,0:T(8,128)(2,1)} %wt_ref.1, bf16[128,768]{1,0:T(8,128)(2,1)} %wg_ref.1), custom_call_target="tpu_custom_call" | custom-call | bytes 500000 | tf_op jit(solution)/shard_map/pallas_call | solution.py:40
  3.0 10.8 %all-to-all-start = ((bf16[4,32,768]{2,1,0:T(8,128)(2,1)}), bf16[4,32,768]{2,1,0:T(8,128)(2,1)S(1)}, u32[]{:S(2)}, u32[]{:S(2)}) async-start(bf16[4,32,768]{2,1,0:T(8,128)(2,1)} %shard_map.189), calls=%async_computation | async-start | bytes 393216 | tf_op jit(solution)/shard_map/all_to_all | solution.py:421
  13.8 0.9 slice_bitcast_fusion
  14.8 4.0 %collective-permute-start = (bf16[2,5,16,512]{3,2,1,0:T(8,128)(2,1)S(1)}, bf16[2,5,16,512]{3,2,1,0:T(8,128)(2,1)S(1)}, u32[]{:S(2)}, u32[]{:S(2)}) collective-permute-start(bf16[2,5,16,512]{3,2,1,0:T(8,128)(2,1)S(1)} %pad_maximum_fusion), channel_id=1, source_target_pairs={{0,4},{4,8},{8,12},{12,16},{16,20},{20,24},{24,28},{28,32},{32,36}... | collective-permute-start | bytes 491528 | tf_op jit(solution)/shard_map/ppermute | solution.py:423
  18.9 2.6 %shard_map.188 = bf16[4,5,16,2304]{3,2,1,0:T(8,128)(2,1)} custom-call(bf16[5,64,512]{2,1,0:T(8,128)(2,1)} %q_ref.3, bf16[5,64,512]{2,1,0:T(8,128)(2,1)} %k_ref.3, bf16[5,64,512]{2,1,0:T(8,128)(2,1)} %v_ref.3, bf16[5,64,768]{2,1,0:T(8,128)(2,1)} %c_ref.5), custom_call_target="tpu_custom_call" | custom-call | bytes 3000000 | tf_op jit(solution)/shard_map/pallas_call | solution.py:40
  21.4 0.0 collective-permute-done.rim_ref
  21.4 0.1 all-to-all-done.rest_0_
  21.5 6.9 %all-to-all-start.1 = ((bf16[4,5,16,2304]{3,2,1,0:T(8,128)(2,1)}), bf16[4,5,16,2304]{3,2,1,0:T(8,128)(2,1)S(1)}, u32[]{:S(2)}, u32[]{:S(2)}) async-start(bf16[4,5,16,2304]{3,2,1,0:T(8,128)(2,1)} %shard_map.188), calls=%async_computation.1 | async-start | bytes 2949120 | tf_op jit(solution)/shard_map/all_to_all | solution.py:432
  28.4 4.5 %collective-permute-start.3 = (bf16[4,32,768]{2,1,0:T(8,128)(2,1)S(1)}, bf16[4,32,768]{2,1,0:T(8,128)(2,1)S(1)}, u32[]{:S(2)}, u32[]{:S(2)}) collective-permute-start(bf16[4,32,768]{2,1,0:T(8,128)(2,1)S(1)} %all-to-all-done.rest_0_), channel_id=1, source_target_pairs={{0,192},{4,196},{8,200},{12,204},{16,208},{20,212},{24,216},{28,22... | collective-permute-start | bytes 589832 | tf_op jit(solution)/shard_map/ppermute | solution.py:448
  32.9 2.4 %collective-permute-start.2 = (bf16[4,32,768]{2,1,0:T(8,128)(2,1)S(1)}, bf16[4,32,768]{2,1,0:T(8,128)(2,1)S(1)}, u32[]{:S(2)}, u32[]{:S(2)}) collective-permute-start(bf16[4,32,768]{2,1,0:T(8,128)(2,1)S(1)} %all-to-all-done.rest_0_), channel_id=1, source_target_pairs={{0,128},{4,132},{8,136},{12,140},{16,144},{20,148},{24,152},{28,15... | collective-permute-start | bytes 589832 | tf_op jit(solution)/shard_map/ppermute | solution.py:448
  35.3 2.5 %collective-permute-start.1 = (bf16[4,32,768]{2,1,0:T(8,128)(2,1)S(1)}, bf16[4,32,768]{2,1,0:T(8,128)(2,1)S(1)}, u32[]{:S(2)}, u32[]{:S(2)}) collective-permute-start(bf16[4,32,768]{2,1,0:T(8,128)(2,1)S(1)} %all-to-all-done.rest_0_), channel_id=1, source_target_pairs={{0,64},{4,68},{8,72},{12,76},{16,80},{20,84},{24,88},{28,92},{32,9... | collective-permute-start | bytes 589832 | tf_op jit(solution)/shard_map/ppermute | solution.py:448
  37.8 0.0 copy-done.8
  37.9 5.1 %shard_map.190 = (f32[5,2,80,256]{3,2,1,0:T(8,128)}, bf16[768,512]{1,0:T(8,128)(2,1)}) custom-call(s32[2]{0:T(128)} %pad_add_fusion.place_ref, s32[8]{0:T(128)} %band_ref.1, bf16[5,64,512]{2,1,0:T(8,128)(2,1)} %q_ref.5, bf16[5,64,512]{2,1,0:T(8,128)(2,1)} %k_ref.5, bf16[5,64,512]{2,1,0:T(8,128)(2,1)} %v_ref.5, bf16[2,5,16,512]{3,2,1,0:T(8,128)(2,1)} %copy-done.8, ...), custom_call_target="tpu_custom_call" | custom-call | flops 2000000000 | bytes 6000000 | tf_op jit(solution)/shard_map/pallas_call | solution.py:40
  43.0 0.0 collective-permute-done.3.rest_3_
  43.0 0.0 collective-permute-done.2.rest_2_
  43.0 0.4 collective-permute-done.1.rest_1_
  43.3 0.0 copy-done.3
  43.3 1.6 %shard_map.191.mine_ref = bf16[4,4,32,768]{3,2,1,0:T(8,128)(2,1)S(1)} custom-call(s32[2]{0:T(128)S(1)} %copy-done.3, bf16[4,32,768]{2,1,0:T(8,128)(2,1)S(1)} %all-to-all-done.rest_0_, bf16[4,32,768]{2,1,0:T(8,128)(2,1)S(1)} %collective-permute-done.1.rest_1_, bf16[4,32,768]{2,1,0:T(8,128)(2,1)S(1)} %collective-permute-done.2.rest_2_, ...), custom_call_target="tpu_custom_call" | custom-call | bytes 1600000 | tf_op jit(solution)/shard_map/pallas_call | solution.py:40
  44.9 0.0 copy-start
  45.0 6.6 %collective-permute-start.4 = (bf16[4,4,32,768]{3,2,1,0:T(8,128)(2,1)S(1)}, bf16[4,4,32,768]{3,2,1,0:T(8,128)(2,1)S(1)}, u32[]{:S(2)}, u32[]{:S(2)}) collective-permute-start(bf16[4,4,32,768]{3,2,1,0:T(8,128)(2,1)S(1)} %shard_map.191.mine_ref), channel_id=1, source_target_pairs={{0,4},{4,0},{8,12},{12,8},{16,20},{20,16},{24,28},{28,24},{32,36},... | collective-permute-start | bytes 2359304 | tf_op jit(solution)/shard_map/ppermute | solution.py:462
  51.5 1.9 %collective-permute-done.4.other_ref = bf16[4,4,32,768]{3,2,1,0:T(8,128)(2,1)S(1)} collective-permute-done((bf16[4,4,32,768]{3,2,1,0:T(8,128)(2,1)S(1)}, bf16[4,4,32,768]{3,2,1,0:T(8,128)(2,1)S(1)}, u32[]{:S(2)}, u32[]{:S(2)}) %collective-permute-start.4) | collective-permute-done | bytes 786464 | tf_op jit(solution)/shard_map/ppermute | solution.py:462
  53.4 0.0 copy-done
  53.4 0.9 copy-done.6
  54.3 7.1 %shard_map.192 = (bf16[5,64,512]{2,1,0:T(8,128)(2,1)}, bf16[5,64,512]{2,1,0:T(8,128)(2,1)}, bf16[5,64,512]{2,1,0:T(8,128)(2,1)}, f32[2,5,16,512]{3,2,1,0:T(8,128)}, bf16[2,5,16,512]{3,2,1,0:T(8,128)(2,1)}) custom-call(s32[2]{0:T(128)} %pad_add_fusion.place_ref, f32[5,2,80,256]{3,2,1,0:T(8,128)} %get-tuple-element.43.prob_ref, bf16[5,64,512]{2,1,0:T(8,128)(2,1)} %q_ref.5, ...), custom_call_target="tpu_custom_call" | custom-call | flops 4000000000 | bytes 6000000 | tf_op jit(solution)/shard_map/pallas_call | solution.py:40
  61.5 2.3 %collective-permute-start.5 = (bf16[2,5,16,512]{3,2,1,0:T(8,128)(2,1)}, bf16[2,5,16,512]{3,2,1,0:T(8,128)(2,1)S(1)}, u32[]{:S(2)}, u32[]{:S(2)}) collective-permute-start(bf16[2,5,16,512]{3,2,1,0:T(8,128)(2,1)} %get-tuple-element.58), channel_id=1, source_target_pairs={{4,0},{8,4},{12,8},{16,12},{20,16},{24,20},{28,24},{32,28},{36,32}... | collective-permute-start | bytes 491528 | tf_op jit(solution)/shard_map/ppermute | solution.py:489
  63.8 0.0 all-to-all-done.1.x_ref
  63.8 0.0 copy-start.5
  63.8 1.1 copy-done.5
  64.9 5.9 %shard_map.193 = (f32[2,2,160,640]{3,2,1,0:T(8,128)}, bf16[768,1024]{1,0:T(8,128)(2,1)}) custom-call(s32[20]{0:T(128)} %group_ref.1, bf16[4,5,16,2304]{3,2,1,0:T(8,128)(2,1)} %copy-done.5, bf16[768,768]{1,0:T(8,128)(2,1)} %constant.13.clone.spread_ref, bf16[768,512]{1,0:T(8,128)(2,1)} %get-tuple-element.51.time_term_ref), custom_call_target="tpu_custom_call" | custom-call | flops 4000000000 | bytes 8000000 | tf_op jit(solution)/shard_map/pallas_call | solution.py:40
  70.8 4.9 %all-to-all-start.2 = ((bf16[8,96,1024]{2,1,0:T(8,128)(2,1)}), bf16[8,96,1024]{2,1,0:T(8,128)(2,1)S(1)}, u32[]{:S(2)}, u32[]{:S(2)}) async-start(bf16[8,96,1024]{2,1,0:T(8,128)(2,1)} %bitcast.9), calls=%async_computation.2 | async-start | bytes 3145728 | tf_op jit(solution)/shard_map/all_to_all | solution.py:508
  75.7 6.6 %shard_map.194 = (bf16[5,16,1536]{2,1,0:T(8,128)(2,1)}, bf16[5,16,1536]{2,1,0:T(8,128)(2,1)}, bf16[5,16,1536]{2,1,0:T(8,128)(2,1)}, bf16[5,16,1536]{2,1,0:T(8,128)(2,1)}) custom-call(s32[2]{0:T(128)} %pad_add_fusion.place_ref, bf16[4,5,16,2304]{3,2,1,0:T(8,128)(2,1)} %copy-done.5, f32[2,2,160,640]{3,2,1,0:T(8,128)} %get-tuple-element.53.prob_ref, ...), custom_call_target="tpu_custom_call" | custom-call | flops 40000000000 | bytes 8000000 | tf_op jit(solution)/shard_map/pallas_call | solution.py:40
  82.3 5.7 %collective-permute-start.6 = (bf16[5,16,1536]{2,1,0:T(8,128)(2,1)}, bf16[5,16,1536]{2,1,0:T(8,128)(2,1)S(1)}, u32[]{:S(2)}, u32[]{:S(2)}) collective-permute-start(bf16[5,16,1536]{2,1,0:T(8,128)(2,1)} %get-tuple-element.63), channel_id=1, source_target_pairs={{0,3},{1,0},{2,1},{3,2},{4,7},{5,4},{6,5},{7,6},{8,11},{9,8},{10,9... | collective-permute-start | bytes 737288 | tf_op jit(solution)/shard_map/ppermute | solution.py:409
  88.0 4.0 %collective-permute-start.7 = (bf16[5,16,1536]{2,1,0:T(8,128)(2,1)}, bf16[5,16,1536]{2,1,0:T(8,128)(2,1)S(1)}, u32[]{:S(2)}, u32[]{:S(2)}) collective-permute-start(bf16[5,16,1536]{2,1,0:T(8,128)(2,1)} %get-tuple-element.64), channel_id=1, source_target_pairs={{0,2},{1,3},{2,0},{3,1},{4,6},{5,7},{6,4},{7,5},{8,10},{9,11},{10,... | collective-permute-start | bytes 737288 | tf_op jit(solution)/shard_map/ppermute | solution.py:409
  92.0 4.0 %collective-permute-start.8 = (bf16[5,16,1536]{2,1,0:T(8,128)(2,1)}, bf16[5,16,1536]{2,1,0:T(8,128)(2,1)S(1)}, u32[]{:S(2)}, u32[]{:S(2)}) collective-permute-start(bf16[5,16,1536]{2,1,0:T(8,128)(2,1)} %get-tuple-element.65), channel_id=1, source_target_pairs={{0,1},{1,2},{2,3},{3,0},{4,5},{5,6},{6,7},{7,4},{8,9},{9,10},{10,1... | collective-permute-start | bytes 737288 | tf_op jit(solution)/shard_map/ppermute | solution.py:409
  96.0 0.4 all-to-all-done.2.in_ref
  96.5 0.0 copy-done.2
  96.5 1.1 shard_map.195
  97.5 12.7 %all-to-all-start.3 = ((bf16[64,16,128]{2,1,0:T(8,128)(2,1)}), bf16[64,16,128]{2,1,0:T(8,128)(2,1)S(1)}, u32[]{:S(2)}, u32[]{:S(2)}) async-start(bf16[64,16,128]{2,1,0:T(8,128)(2,1)} %shard_map.195), calls=%async_computation.3 | async-start | bytes 524288 | tf_op jit(solution)/shard_map/all_to_all | solution.py:565
  110.3 0.0 collective-permute-done.5.got_ref
  110.3 0.7 copy-done.7
  110.9 1.7 %shard_map.196 = (bf16[5,64,512]{2,1,0:T(8,128)(2,1)}, bf16[5,64,512]{2,1,0:T(8,128)(2,1)}) custom-call(bf16[5,64,512]{2,1,0:T(8,128)(2,1)} %get-tuple-element.48.gk_any, bf16[5,64,512]{2,1,0:T(8,128)(2,1)} %get-tuple-element.49.gv_any, f32[2,5,16,512]{3,2,1,0:T(8,128)} %get-tuple-element.57.tail_ref, ...), custom_call_target="tpu_custom_call", output_to_operand_aliasing={{0}: (0, {}), {1}: (1, {})} | custom-call | flops 40000000000 | bytes 1000000 | tf_op jit(solution)/shard_map/pallas_call | solution.py:543
  112.7 0.0 collective-permute-done.6.rest_1_
  112.7 0.0 collective-permute-done.7.rest_2_
  112.7 0.0 collective-permute-done.8.rest_3_
  112.7 1.6 %shard_map.197 = (bf16[5,64,512]{2,1,0:T(8,128)(2,1)}, bf16[5,64,512]{2,1,0:T(8,128)(2,1)}, bf16[5,64,512]{2,1,0:T(8,128)(2,1)}) custom-call(s32[2]{0:T(128)S(1)} %copy-done.4, bf16[5,16,1536]{2,1,0:T(8,128)(2,1)S(1)} %copy-done.1, bf16[5,16,1536]{2,1,0:T(8,128)(2,1)S(1)} %collective-permute-done.6.rest_1_, ...), custom_call_target="tpu_custom_call" | custom-call | bytes 2000000 | tf_op jit(solution)/shard_map/pallas_call | solution.py:40
  114.3 10.1 %all-to-all-done.3.in_ref = bf16[64,16,128]{2,1,0:T(8,128)(2,1)S(1)} async-done(((bf16[64,16,128]{2,1,0:T(8,128)(2,1)}), bf16[64,16,128]{2,1,0:T(8,128)(2,1)S(1)}, u32[]{:S(2)}, u32[]{:S(2)}) %all-to-all-start.3) | async-done | bytes 262176 | tf_op jit(solution)/shard_map/all_to_all | solution.py:565
  124.4 0.7 shard_map.198
  (10 shorter events, 0.0 us)
Async XLA Ops:
  3.0 18.5 %all-to-all-start = ((bf16[4,32,768]{2,1,0:T(8,128)(2,1)}), bf16[4,32,768]{2,1,0:T(8,128)(2,1)S(1)}, u32[]{:S(2)}, u32[]{:S(2)}) async-start(bf16[4,32,768]{2,1,0:T(8,128)(2,1)} %shard_map.189), calls=%async_computation | async-start | bytes 393216 | tf_op jit(solution)/shard_map/all_to_all | solution.py:421
  14.8 6.6 %collective-permute-start = (bf16[2,5,16,512]{3,2,1,0:T(8,128)(2,1)S(1)}, bf16[2,5,16,512]{3,2,1,0:T(8,128)(2,1)S(1)}, u32[]{:S(2)}, u32[]{:S(2)}) collective-permute-start(bf16[2,5,16,512]{3,2,1,0:T(8,128)(2,1)S(1)} %pad_maximum_fusion), channel_id=1, source_target_pairs={{0,4},{4,8},{8,12},{12,16},{16,20},{20,24},{24,28},{28,32},{32,36}... | collective-permute-start | bytes 491528 | tf_op jit(solution)/shard_map/ppermute | solution.py:423
  21.4 16.4 %copy-start.8 = (bf16[2,5,16,512]{3,2,1,0:T(8,128)(2,1)}, bf16[2,5,16,512]{3,2,1,0:T(8,128)(2,1)S(1)}, u32[]{:S(2)}) copy-start(bf16[2,5,16,512]{3,2,1,0:T(8,128)(2,1)S(1)} %collective-permute-done.rim_ref) | copy-start | bytes 491524
  21.5 42.2 %all-to-all-start.1 = ((bf16[4,5,16,2304]{3,2,1,0:T(8,128)(2,1)}), bf16[4,5,16,2304]{3,2,1,0:T(8,128)(2,1)S(1)}, u32[]{:S(2)}, u32[]{:S(2)}) async-start(bf16[4,5,16,2304]{3,2,1,0:T(8,128)(2,1)} %shard_map.188), calls=%async_computation.1 | async-start | bytes 2949120 | tf_op jit(solution)/shard_map/all_to_all | solution.py:432
  28.4 15.0 %copy-start.3 = (s32[2]{0:T(128)S(1)}, s32[2]{0:T(128)}, u32[]{:S(2)}) copy-start(s32[2]{0:T(128)} %pad_add_fusion.place_ref) | copy-start | bytes 28
  28.4 14.6 %collective-permute-start.3 = (bf16[4,32,768]{2,1,0:T(8,128)(2,1)S(1)}, bf16[4,32,768]{2,1,0:T(8,128)(2,1)S(1)}, u32[]{:S(2)}, u32[]{:S(2)}) collective-permute-start(bf16[4,32,768]{2,1,0:T(8,128)(2,1)S(1)} %all-to-all-done.rest_0_), channel_id=1, source_target_pairs={{0,192},{4,196},{8,200},{12,204},{16,208},{20,212},{24,216},{28,22... | collective-permute-start | bytes 589832 | tf_op jit(solution)/shard_map/ppermute | solution.py:448
  32.9 10.1 %collective-permute-start.2 = (bf16[4,32,768]{2,1,0:T(8,128)(2,1)S(1)}, bf16[4,32,768]{2,1,0:T(8,128)(2,1)S(1)}, u32[]{:S(2)}, u32[]{:S(2)}) collective-permute-start(bf16[4,32,768]{2,1,0:T(8,128)(2,1)S(1)} %all-to-all-done.rest_0_), channel_id=1, source_target_pairs={{0,128},{4,132},{8,136},{12,140},{16,144},{20,148},{24,152},{28,15... | collective-permute-start | bytes 589832 | tf_op jit(solution)/shard_map/ppermute | solution.py:448
  35.3 8.0 %collective-permute-start.1 = (bf16[4,32,768]{2,1,0:T(8,128)(2,1)S(1)}, bf16[4,32,768]{2,1,0:T(8,128)(2,1)S(1)}, u32[]{:S(2)}, u32[]{:S(2)}) collective-permute-start(bf16[4,32,768]{2,1,0:T(8,128)(2,1)S(1)} %all-to-all-done.rest_0_), channel_id=1, source_target_pairs={{0,64},{4,68},{8,72},{12,76},{16,80},{20,84},{24,88},{28,92},{32,9... | collective-permute-start | bytes 589832 | tf_op jit(solution)/shard_map/ppermute | solution.py:448
  44.9 8.5 %copy-start = (bf16[4,4,32,768]{3,2,1,0:T(8,128)(2,1)}, bf16[4,4,32,768]{3,2,1,0:T(8,128)(2,1)S(1)}, u32[]{:S(2)}) copy-start(bf16[4,4,32,768]{3,2,1,0:T(8,128)(2,1)S(1)} %shard_map.191.mine_ref) | copy-start | bytes 2359300
  45.0 8.5 %collective-permute-start.4 = (bf16[4,4,32,768]{3,2,1,0:T(8,128)(2,1)S(1)}, bf16[4,4,32,768]{3,2,1,0:T(8,128)(2,1)S(1)}, u32[]{:S(2)}, u32[]{:S(2)}) collective-permute-start(bf16[4,4,32,768]{3,2,1,0:T(8,128)(2,1)S(1)} %shard_map.191.mine_ref), channel_id=1, source_target_pairs={{0,4},{4,0},{8,12},{12,8},{16,20},{20,16},{24,28},{28,24},{32,36},... | collective-permute-start | bytes 2359304 | tf_op jit(solution)/shard_map/ppermute | solution.py:462
  53.4 0.9 copy-start.6
  61.5 48.8 %collective-permute-start.5 = (bf16[2,5,16,512]{3,2,1,0:T(8,128)(2,1)}, bf16[2,5,16,512]{3,2,1,0:T(8,128)(2,1)S(1)}, u32[]{:S(2)}, u32[]{:S(2)}) collective-permute-start(bf16[2,5,16,512]{3,2,1,0:T(8,128)(2,1)} %get-tuple-element.58), channel_id=1, source_target_pairs={{4,0},{8,4},{12,8},{16,12},{20,16},{24,20},{28,24},{32,28},{36,32}... | collective-permute-start | bytes 491528 | tf_op jit(solution)/shard_map/ppermute | solution.py:489
  63.8 1.1 copy-start.5
  70.8 25.6 %all-to-all-start.2 = ((bf16[8,96,1024]{2,1,0:T(8,128)(2,1)}), bf16[8,96,1024]{2,1,0:T(8,128)(2,1)S(1)}, u32[]{:S(2)}, u32[]{:S(2)}) async-start(bf16[8,96,1024]{2,1,0:T(8,128)(2,1)} %bitcast.9), calls=%async_computation.2 | async-start | bytes 3145728 | tf_op jit(solution)/shard_map/all_to_all | solution.py:508
  75.7 20.7 %copy-start.2 = (bf16[128,96]{1,0:T(8,128)(2,1)S(1)}, bf16[128,96]{1,0:T(8,128)(2,1)}, u32[]{:S(2)}) copy-start(bf16[128,96]{1,0:T(8,128)(2,1)} %constant.14.clone.pad_ref) | copy-start | bytes 73732
  82.3 30.4 %collective-permute-start.6 = (bf16[5,16,1536]{2,1,0:T(8,128)(2,1)}, bf16[5,16,1536]{2,1,0:T(8,128)(2,1)S(1)}, u32[]{:S(2)}, u32[]{:S(2)}) collective-permute-start(bf16[5,16,1536]{2,1,0:T(8,128)(2,1)} %get-tuple-element.63), channel_id=1, source_target_pairs={{0,3},{1,0},{2,1},{3,2},{4,7},{5,4},{6,5},{7,6},{8,11},{9,8},{10,9... | collective-permute-start | bytes 737288 | tf_op jit(solution)/shard_map/ppermute | solution.py:409
  88.0 24.7 %collective-permute-start.7 = (bf16[5,16,1536]{2,1,0:T(8,128)(2,1)}, bf16[5,16,1536]{2,1,0:T(8,128)(2,1)S(1)}, u32[]{:S(2)}, u32[]{:S(2)}) collective-permute-start(bf16[5,16,1536]{2,1,0:T(8,128)(2,1)} %get-tuple-element.64), channel_id=1, source_target_pairs={{0,2},{1,3},{2,0},{3,1},{4,6},{5,7},{6,4},{7,5},{8,10},{9,11},{10,... | collective-permute-start | bytes 737288 | tf_op jit(solution)/shard_map/ppermute | solution.py:409
  92.0 20.7 %collective-permute-start.8 = (bf16[5,16,1536]{2,1,0:T(8,128)(2,1)}, bf16[5,16,1536]{2,1,0:T(8,128)(2,1)S(1)}, u32[]{:S(2)}, u32[]{:S(2)}) collective-permute-start(bf16[5,16,1536]{2,1,0:T(8,128)(2,1)} %get-tuple-element.65), channel_id=1, source_target_pairs={{0,1},{1,2},{2,3},{3,0},{4,5},{5,6},{6,7},{7,4},{8,9},{9,10},{10,1... | collective-permute-start | bytes 737288 | tf_op jit(solution)/shard_map/ppermute | solution.py:409
  97.5 26.9 %all-to-all-start.3 = ((bf16[64,16,128]{2,1,0:T(8,128)(2,1)}), bf16[64,16,128]{2,1,0:T(8,128)(2,1)S(1)}, u32[]{:S(2)}, u32[]{:S(2)}) async-start(bf16[64,16,128]{2,1,0:T(8,128)(2,1)} %shard_map.195), calls=%async_computation.3 | async-start | bytes 524288 | tf_op jit(solution)/shard_map/all_to_all | solution.py:565
  110.3 0.7 copy-start.7
  110.9 1.8 %copy-start.1 = (bf16[5,16,1536]{2,1,0:T(8,128)(2,1)S(1)}, bf16[5,16,1536]{2,1,0:T(8,128)(2,1)}, u32[]{:S(2)}) copy-start(bf16[5,16,1536]{2,1,0:T(8,128)(2,1)} %get-tuple-element.54.rest_0_) | copy-start | bytes 737284
  110.9 1.8 %copy-start.4 = (s32[2]{0:T(128)S(1)}, s32[2]{0:T(128)}, u32[]{:S(2)}) copy-start(s32[2]{0:T(128)} %pad_add_fusion.place_ref) | copy-start | bytes 28
where the time goes:
time: 126 us; the launch traced here: 125 us
  starting transfers between devices  71.3 us (57%)
  Pallas kernels  35.7 us (28%)
  waiting for transfers between devices  12.9 us (10%)
  local copies, waits for them, and re-layouts  3.65 us (3%)
    pallas_call x10, Pallas kernels, call(): pl.pallas_call(body, out_shape=out_shape, grid=(1,), in_specs=[block(o, '...  34 us
    ppermute x3, starting transfers between devices, over_series(): lax.ppermute(value, 'series', [(j, (j + shift) % parts) for j in range(pa...  13.6 us
    all_to_all x1, starting transfers between devices, per_device(): lax.all_to_all(chunks, ('series', 'tm'), 0, 0, tiled=True, axis_index_gro...  12.7 us
    all_to_all x1, starting transfers between devices, per_device(): column_piece = lax.all_to_all(piece, 'series', 0, 0, tiled=True)  10.8 us
    all_to_all x1, waiting for transfers between devices, per_device(): lax.all_to_all(chunks, ('series', 'tm'), 0, 0, tiled=True, axis_index_gro...  10.1 us
    ppermute x3, starting transfers between devices, per_device(): lax.ppermute(column_piece, 'tm', along_x(shift))  9.45 us
    all_to_all x1, starting transfers between devices, per_device(): moved = lax.all_to_all(packed, 'series', 0, 0, tiled=True)  6.85 us
    ppermute x1, starting transfers between devices, per_device(): lax.ppermute(weight_mine, 'tm', [(i, i ^ 1) for i in range(count)])  6.58 us
  transfers between devices with their start and end apart: 13, of which 5 were waited for; matrix products, arithmetic and copies ran while one was open for 1% of the time, Pallas kernels for 27%

commit v1 on v0

--- a/solution.py
+++ b/solution.py
@@ -428,7 +428,7 @@
         0,
         3_000_000,
     )
-    packed, column_piece, rim = lax.optimization_barrier((packed, column_piece, rim))
+    packed, column_piece = lax.optimization_barrier((packed, column_piece))
     moved = lax.all_to_all(packed, "series", 0, 0, tiled=True)
     spread = spread_matrix(model, count)
     quads = width // (QUAD * HEAD_DIM)
@@ -461,33 +461,6 @@
     )
     weight_other = lax.ppermute(weight_mine, "tm", [(i, i ^ 1) for i in range(count)])
 
-    grad_tq, grad_tk, grad_tv, tail, rim_grad = call(
-        time_backward_body,
-        (
-            shape((ser, rows, width), BF16),
-            shape((ser, rows, width), BF16),
-            shape((ser, rows, width), BF16),
-            shape((2, ser, BAND, width), F32),
-            shape((2, ser, BAND, width), BF16),
-        ),
-        (
-            where,
-            prob,
-            time_query,
-            time_key,
-            time_value,
-            rim,
-            cotangent,
-            weight_mine,
-            weight_other,
-        ),
-        4_000_000_000,
-        6_000_000,
-        smem=(0,),
-        scratch=[pltpu.VMEM((ser * rows, width), BF16), pltpu.VMEM((width, model), BF16)],
-    )
-    rim_back = lax.ppermute(rim_grad, "tm", [(i + 1, i) for i in range(count - 1)])
-    term_time, grad_tq = lax.optimization_barrier((term_time, grad_tq))
     total = parts * ser * patches
     group_prob, term = call(
         functools.partial(group_forward_body, scale),
@@ -526,7 +499,6 @@
             pltpu.VMEM((parts * ser, patches, 3 * width), F32),
         ],
     )
-    plane, _ = lax.optimization_barrier((plane, back[0]))
     second = parts * Y_SIZE * LOW_SIZE
     chunks = call(
         first_sum_body,
@@ -538,7 +510,45 @@
     )
     returned = [back[0]] + [over_series(back[shift], -shift) for shift in range(1, parts)]
 
-    chunks, tail = lax.optimization_barrier((chunks, tail))
+    chunks, order, _ = lax.optimization_barrier((chunks, where, back[0]))
+    grad_tq, grad_tk, grad_tv, tail, rim_grad = call(
+        time_backward_body,
+        (
+            shape((ser, rows, width), BF16),
+            shape((ser, rows, width), BF16),
+            shape((ser, rows, width), BF16),
+            shape((2, ser, BAND, width), F32),
+            shape((2, ser, BAND, width), BF16),
+        ),
+        (
+            order,
+            prob,
+            time_query,
+            time_key,
+            time_value,
+            rim,
+            cotangent,
+            weight_mine,
+            weight_other,
+        ),
+        40_000_000_000,
+        6_000_000,
+        smem=(0,),
+        scratch=[pltpu.VMEM((ser * rows, width), BF16), pltpu.VMEM((width, model), BF16)],
+    )
+    rim_back = lax.ppermute(rim_grad, "tm", [(i + 1, i) for i in range(count - 1)])
+    grad_gq, grad_gk, grad_gv = call(
+        unpack_body,
+        (shape((ser, rows, width), BF16),) * 3,
+        (where, *returned),
+        0,
+        2_000_000,
+        smem=(0,),
+        anywhere=True,
+        scratch=[sem((3 * parts,))],
+        room=8192,
+    )
+    rim_back, grad_gq = lax.optimization_barrier((rim_back, grad_gq))
     border = pl.BlockSpec((ser, BAND, width), lambda i: (0, rows // BAND - 1, 0))
     grad_tk, grad_tv = pl.pallas_call(
         time_join_body,
@@ -548,20 +558,8 @@
         out_specs=[border] * 2,
         input_output_aliases={0: 0, 1: 1},
         compiler_params=pltpu.CompilerParams(vmem_limit_bytes=60 * 1024 * 1024),
-        cost_estimate=pl.CostEstimate(flops=40_000_000_000, bytes_accessed=1_000_000, transcendentals=0),
+        cost_estimate=pl.CostEstimate(flops=0, bytes_accessed=1_000_000, transcendentals=0),
     )(grad_tk, grad_tv, tail, rim_back)
-    order, grad_tk = lax.optimization_barrier((where, grad_tk))
-    grad_gq, grad_gk, grad_gv = call(
-        unpack_body,
-        (shape((ser, rows, width), BF16),) * 3,
-        (order, *returned),
-        0,
-        2_000_000,
-        smem=(0,),
-        anywhere=True,
-        scratch=[sem((3 * parts,))],
-        room=8192,
-    )
     chunks = lax.all_to_all(
         chunks,
         ("series", "tm"),

time: 126 us -> 124 us (0.984)
  waiting for transfers between devices: 12.9 us -> 9.43 us
  starting transfers between devices: 71.3 us -> 73.2 us
    all_to_all x1, waiting for transfers between devices: 10.1 us -> 0.01 us  [per_device(): lax.all_to_all(chunks, ('series', 'tm'), 0, 0, tiled=True, axis_index_gro...]
    all_to_all x1, starting transfers between devices: 4.92 us -> 14.2 us  [per_device(): lax.all_to_all(term.reshape(first, model // first, 2 * width), 'tm', 0, 0...]
    all_to_all x1, waiting for transfers between devices: 0.08 us -> 5.11 us  [per_device(): column_piece = lax.all_to_all(piece, 'series', 0, 0, tiled=True)]
    ppermute x1, starting transfers between devices: 6.58 us -> 1.93 us  [per_device(): lax.ppermute(weight_mine, 'tm', [(i, i ^ 1) for i in range(count)])]
    all_to_all x1, starting transfers between devices: 6.85 us -> 3.76 us  [per_device(): moved = lax.all_to_all(packed, 'series', 0, 0, tiled=True)]
    ppermute x1, waiting for transfers between devices: 0.01 us -> 2.85 us  [per_device(): lax.ppermute(rim_grad, 'tm', [(i + 1, i) for i in range(count - 1)])]
    all_to_all x1, starting transfers between devices: 12.7 us -> 10.1 us  [per_device(): lax.all_to_all(chunks, ('series', 'tm'), 0, 0, tiled=True, axis_index_gro...]
    ppermute x1, starting transfers between devices: 4.05 us -> 6.12 us  [per_device(): rim = lax.ppermute(rim, 'tm', [(i, i + 1) for i in range(count - 1)])]
  transfers between devices with their start and end apart: 13 -> 13, of which waited for: 5 -> 3; matrix products, arithmetic and copies ran while one was open for 1% -> 1% of each run, Pallas kernels for 27% -> 27%
where the time goes in v1:
time: 124 us; the launch traced here: 123 us
  starting transfers between devices  73.2 us (59%)
  Pallas kernels  35.7 us (29%)
  waiting for transfers between devices  9.43 us (8%)
  local copies, waits for them, and re-layouts  3.42 us (3%)
    pallas_call x10, Pallas kernels, call(): pl.pallas_call(body, out_shape=out_shape, grid=(1,), in_specs=[block(o, '...  34 us
    all_to_all x1, starting transfers between devices, per_device(): lax.all_to_all(term.reshape(first, model // first, 2 * width), 'tm', 0, 0...  14.2 us
    ppermute x3, starting transfers between devices, over_series(): lax.ppermute(value, 'series', [(j, (j + shift) % parts) for j in range(pa...  12.7 us
    all_to_all x1, starting transfers between devices, per_device(): column_piece = lax.all_to_all(piece, 'series', 0, 0, tiled=True)  10.8 us
    ppermute x3, starting transfers between devices, per_device(): lax.ppermute(column_piece, 'tm', along_x(shift))  10.5 us
    all_to_all x1, starting transfers between devices, per_device(): lax.all_to_all(chunks, ('series', 'tm'), 0, 0, tiled=True, axis_index_gro...  10.1 us
    ppermute x1, starting transfers between devices, per_device(): rim = lax.ppermute(rim, 'tm', [(i, i + 1) for i in range(count - 1)])  6.12 us
    all_to_all x1, waiting for transfers between devices, per_device(): column_piece = lax.all_to_all(piece, 'series', 0, 0, tiled=True)  5.11 us
  transfers between devices with their start and end apart: 13, of which 3 were waited for; matrix products, arithmetic and copies ran while one was open for 1% of the time, Pallas kernels for 27%

profile of v1, /device:TPU:1, one launch (start us, length us, event | category | flops | bytes accessed | tf_op | source)
XLA Modules:
  0.0 123.3 jit_solution(9477213495922822173)
XLA Ops:
  0.6 0.6 pad_add_fusion.place_ref
  1.3 1.7 %shard_map.189 = bf16[4,32,768]{2,1,0:T(8,128)(2,1)} custom-call(s32[2]{0:T(128)} %pad_add_fusion.place_ref, bf16[128,768]{1,0:T(8,128)(2,1)} %wt_ref.1, bf16[128,768]{1,0:T(8,128)(2,1)} %wg_ref.1), custom_call_target="tpu_custom_call" | custom-call | bytes 500000 | tf_op jit(solution)/shard_map/pallas_call | solution.py:40
  3.0 10.8 %all-to-all-start = ((bf16[4,32,768]{2,1,0:T(8,128)(2,1)}), bf16[4,32,768]{2,1,0:T(8,128)(2,1)S(1)}, u32[]{:S(2)}, u32[]{:S(2)}) async-start(bf16[4,32,768]{2,1,0:T(8,128)(2,1)} %shard_map.189), calls=%async_computation | async-start | bytes 393216 | tf_op jit(solution)/shard_map/all_to_all | solution.py:421
  13.9 2.6 %shard_map.188 = bf16[4,5,16,2304]{3,2,1,0:T(8,128)(2,1)} custom-call(bf16[5,64,512]{2,1,0:T(8,128)(2,1)} %q_ref.3, bf16[5,64,512]{2,1,0:T(8,128)(2,1)} %k_ref.3, bf16[5,64,512]{2,1,0:T(8,128)(2,1)} %v_ref.3, bf16[5,64,768]{2,1,0:T(8,128)(2,1)} %c_ref.5), custom_call_target="tpu_custom_call" | custom-call | bytes 3000000 | tf_op jit(solution)/shard_map/pallas_call | solution.py:40
  16.4 5.1 %all-to-all-done.rest_0_ = bf16[4,32,768]{2,1,0:T(8,128)(2,1)S(1)} async-done(((bf16[4,32,768]{2,1,0:T(8,128)(2,1)}), bf16[4,32,768]{2,1,0:T(8,128)(2,1)S(1)}, u32[]{:S(2)}, u32[]{:S(2)}) %all-to-all-start) | async-done | bytes 196640 | tf_op jit(solution)/shard_map/all_to_all | solution.py:421
  21.5 3.8 %all-to-all-start.1 = ((bf16[4,5,16,2304]{3,2,1,0:T(8,128)(2,1)}), bf16[4,5,16,2304]{3,2,1,0:T(8,128)(2,1)S(1)}, u32[]{:S(2)}, u32[]{:S(2)}) async-start(bf16[4,5,16,2304]{3,2,1,0:T(8,128)(2,1)} %shard_map.188), calls=%async_computation.1 | async-start | bytes 2949120 | tf_op jit(solution)/shard_map/all_to_all | solution.py:432
  25.3 0.9 slice_bitcast_fusion
  26.3 0.0 copy-start.3
  26.3 6.1 %collective-permute-start = (bf16[2,5,16,512]{3,2,1,0:T(8,128)(2,1)S(1)}, bf16[2,5,16,512]{3,2,1,0:T(8,128)(2,1)S(1)}, u32[]{:S(2)}, u32[]{:S(2)}) collective-permute-start(bf16[2,5,16,512]{3,2,1,0:T(8,128)(2,1)S(1)} %pad_maximum_fusion), channel_id=1, source_target_pairs={{0,4},{4,8},{8,12},{12,16},{16,20},{20,24},{24,28},{28,32},{32,36}... | collective-permute-start | bytes 491528 | tf_op jit(solution)/shard_map/ppermute | solution.py:423
  32.4 3.1 %collective-permute-start.1 = (bf16[4,32,768]{2,1,0:T(8,128)(2,1)S(1)}, bf16[4,32,768]{2,1,0:T(8,128)(2,1)S(1)}, u32[]{:S(2)}, u32[]{:S(2)}) collective-permute-start(bf16[4,32,768]{2,1,0:T(8,128)(2,1)S(1)} %all-to-all-done.rest_0_), channel_id=1, source_target_pairs={{0,64},{4,68},{8,72},{12,76},{16,80},{20,84},{24,88},{28,92},{32,9... | collective-permute-start | bytes 589832 | tf_op jit(solution)/shard_map/ppermute | solution.py:448
  35.5 4.4 %collective-permute-start.2 = (bf16[4,32,768]{2,1,0:T(8,128)(2,1)S(1)}, bf16[4,32,768]{2,1,0:T(8,128)(2,1)S(1)}, u32[]{:S(2)}, u32[]{:S(2)}) collective-permute-start(bf16[4,32,768]{2,1,0:T(8,128)(2,1)S(1)} %all-to-all-done.rest_0_), channel_id=1, source_target_pairs={{0,128},{4,132},{8,136},{12,140},{16,144},{20,148},{24,152},{28,15... | collective-permute-start | bytes 589832 | tf_op jit(solution)/shard_map/ppermute | solution.py:448
  39.9 3.1 %collective-permute-start.3 = (bf16[4,32,768]{2,1,0:T(8,128)(2,1)S(1)}, bf16[4,32,768]{2,1,0:T(8,128)(2,1)S(1)}, u32[]{:S(2)}, u32[]{:S(2)}) collective-permute-start(bf16[4,32,768]{2,1,0:T(8,128)(2,1)S(1)} %all-to-all-done.rest_0_), channel_id=1, source_target_pairs={{0,192},{4,196},{8,200},{12,204},{16,208},{20,212},{24,216},{28,22... | collective-permute-start | bytes 589832 | tf_op jit(solution)/shard_map/ppermute | solution.py:448
  43.0 0.0 collective-permute-done.rim_ref
  43.0 0.0 copy-start.7
  43.0 0.7 copy-done.7
  43.7 5.1 %shard_map.190 = (f32[5,2,80,256]{3,2,1,0:T(8,128)}, bf16[768,512]{1,0:T(8,128)(2,1)}) custom-call(s32[2]{0:T(128)} %pad_add_fusion.place_ref, s32[8]{0:T(128)} %band_ref.1, bf16[5,64,512]{2,1,0:T(8,128)(2,1)} %q_ref.5, bf16[5,64,512]{2,1,0:T(8,128)(2,1)} %k_ref.5, bf16[5,64,512]{2,1,0:T(8,128)(2,1)} %v_ref.5, bf16[2,5,16,512]{3,2,1,0:T(8,128)(2,1)} %copy-done.7, ...), custom_call_target="tpu_custom_call" | custom-call | flops 2000000000 | bytes 6000000 | tf_op jit(solution)/shard_map/pallas_call | solution.py:40
  48.8 0.0 collective-permute-done.1.rest_1_
  48.8 0.0 collective-permute-done.2.rest_2_
  48.8 0.0 collective-permute-done.3.rest_3_
  48.8 0.0 copy-done.3
  48.8 1.6 %shard_map.193.mine_ref = bf16[4,4,32,768]{3,2,1,0:T(8,128)(2,1)S(1)} custom-call(s32[2]{0:T(128)S(1)} %copy-done.3, bf16[4,32,768]{2,1,0:T(8,128)(2,1)S(1)} %all-to-all-done.rest_0_, bf16[4,32,768]{2,1,0:T(8,128)(2,1)S(1)} %collective-permute-done.1.rest_1_, bf16[4,32,768]{2,1,0:T(8,128)(2,1)S(1)} %collective-permute-done.2.rest_2_, ...), custom_call_target="tpu_custom_call" | custom-call | bytes 1600000 | tf_op jit(solution)/shard_map/pallas_call | solution.py:40
  50.4 0.0 copy-start
  50.4 1.9 %collective-permute-start.4 = (bf16[4,4,32,768]{3,2,1,0:T(8,128)(2,1)S(1)}, bf16[4,4,32,768]{3,2,1,0:T(8,128)(2,1)}, u32[]{:S(2)}, u32[]{:S(2)}) collective-permute-start(bf16[4,4,32,768]{3,2,1,0:T(8,128)(2,1)S(1)} %shard_map.193.mine_ref), channel_id=1, source_target_pairs={{0,4},{4,0},{8,12},{12,8},{16,20},{20,16},{24,28},{28,24},{32,36},... | collective-permute-start | bytes 2359304 | tf_op jit(solution)/shard_map/ppermute | solution.py:462
  52.4 0.0 all-to-all-done.1.x_ref
  52.4 0.0 copy-start.5
  52.4 1.1 copy-done.5
  53.5 5.9 %shard_map.191 = (f32[2,2,160,640]{3,2,1,0:T(8,128)}, bf16[768,1024]{1,0:T(8,128)(2,1)}) custom-call(s32[20]{0:T(128)} %group_ref.1, bf16[4,5,16,2304]{3,2,1,0:T(8,128)(2,1)} %copy-done.5, bf16[768,768]{1,0:T(8,128)(2,1)} %constant.13.clone.spread_ref, bf16[768,512]{1,0:T(8,128)(2,1)} %get-tuple-element.38.time_term_ref), custom_call_target="tpu_custom_call" | custom-call | flops 4000000000 | bytes 8000000 | tf_op jit(solution)/shard_map/pallas_call | solution.py:40
  59.4 14.2 %all-to-all-start.2 = ((bf16[8,96,1024]{2,1,0:T(8,128)(2,1)}), bf16[8,96,1024]{2,1,0:T(8,128)(2,1)S(1)}, u32[]{:S(2)}, u32[]{:S(2)}) async-start(bf16[8,96,1024]{2,1,0:T(8,128)(2,1)} %bitcast.9), calls=%async_computation.2 | async-start | bytes 3145728 | tf_op jit(solution)/shard_map/all_to_all | solution.py:481
  73.6 0.0 collective-permute-done.4.other_ref
  73.6 6.6 %shard_map.194 = (bf16[5,16,1536]{2,1,0:T(8,128)(2,1)}, bf16[5,16,1536]{2,1,0:T(8,128)(2,1)}, bf16[5,16,1536]{2,1,0:T(8,128)(2,1)}, bf16[5,16,1536]{2,1,0:T(8,128)(2,1)}) custom-call(s32[2]{0:T(128)} %pad_add_fusion.place_ref, bf16[4,5,16,2304]{3,2,1,0:T(8,128)(2,1)} %copy-done.5, f32[2,2,160,640]{3,2,1,0:T(8,128)} %get-tuple-element.40.prob_ref, ...), custom_call_target="tpu_custom_call" | custom-call | flops 40000000000 | bytes 8000000 | tf_op jit(solution)/shard_map/pallas_call | solution.py:40
  80.2 5.5 %collective-permute-start.6 = (bf16[5,16,1536]{2,1,0:T(8,128)(2,1)}, bf16[5,16,1536]{2,1,0:T(8,128)(2,1)S(1)}, u32[]{:S(2)}, u32[]{:S(2)}) collective-permute-start(bf16[5,16,1536]{2,1,0:T(8,128)(2,1)} %get-tuple-element.51), channel_id=1, source_target_pairs={{0,3},{1,0},{2,1},{3,2},{4,7},{5,4},{6,5},{7,6},{8,11},{9,8},{10,9... | collective-permute-start | bytes 737288 | tf_op jit(solution)/shard_map/ppermute | solution.py:409
  85.7 5.2 %collective-permute-start.7 = (bf16[5,16,1536]{2,1,0:T(8,128)(2,1)}, bf16[5,16,1536]{2,1,0:T(8,128)(2,1)S(1)}, u32[]{:S(2)}, u32[]{:S(2)}) collective-permute-start(bf16[5,16,1536]{2,1,0:T(8,128)(2,1)} %get-tuple-element.52), channel_id=1, source_target_pairs={{0,2},{1,3},{2,0},{3,1},{4,6},{5,7},{6,4},{7,5},{8,10},{9,11},{10,... | collective-permute-start | bytes 737288 | tf_op jit(solution)/shard_map/ppermute | solution.py:409
  91.0 1.9 %collective-permute-start.8 = (bf16[5,16,1536]{2,1,0:T(8,128)(2,1)}, bf16[5,16,1536]{2,1,0:T(8,128)(2,1)S(1)}, u32[]{:S(2)}, u32[]{:S(2)}) collective-permute-start(bf16[5,16,1536]{2,1,0:T(8,128)(2,1)} %get-tuple-element.53), channel_id=1, source_target_pairs={{0,1},{1,2},{2,3},{3,0},{4,5},{5,6},{6,7},{7,4},{8,9},{9,10},{10,1... | collective-permute-start | bytes 737288 | tf_op jit(solution)/shard_map/ppermute | solution.py:409
  92.9 1.4 %all-to-all-done.2.in_ref = bf16[8,96,1024]{2,1,0:T(8,128)(2,1)S(1)} async-done(((bf16[8,96,1024]{2,1,0:T(8,128)(2,1)}), bf16[8,96,1024]{2,1,0:T(8,128)(2,1)S(1)}, u32[]{:S(2)}, u32[]{:S(2)}) %all-to-all-start.2) | async-done | bytes 1572896 | tf_op jit(solution)/shard_map/all_to_all | solution.py:481
  94.3 1.1 shard_map.192
  95.4 10.1 %all-to-all-start.3 = ((bf16[64,16,128]{2,1,0:T(8,128)(2,1)}), bf16[64,16,128]{2,1,0:T(8,128)(2,1)S(1)}, u32[]{:S(2)}, u32[]{:S(2)}) async-start(bf16[64,16,128]{2,1,0:T(8,128)(2,1)} %shard_map.192), calls=%async_computation.3 | async-start | bytes 524288 | tf_op jit(solution)/shard_map/all_to_all | solution.py:563
  105.5 0.0 copy-start.1
  105.5 7.2 %shard_map.195 = (bf16[5,64,512]{2,1,0:T(8,128)(2,1)}, bf16[5,64,512]{2,1,0:T(8,128)(2,1)}, bf16[5,64,512]{2,1,0:T(8,128)(2,1)}, f32[2,5,16,512]{3,2,1,0:T(8,128)}, bf16[2,5,16,512]{3,2,1,0:T(8,128)(2,1)}) custom-call(s32[2]{0:T(128)} %pad_add_fusion.place_ref, f32[5,2,80,256]{3,2,1,0:T(8,128)} %get-tuple-element.45.prob_ref, bf16[5,64,512]{2,1,0:T(8,128)(2,1)} %q_ref.5, ...), custom_call_target="tpu_custom_call" | custom-call | flops 40000000000 | bytes 6000000 | tf_op jit(solution)/shard_map/pallas_call | solution.py:40
  112.7 3.1 %collective-permute-start.5 = (bf16[2,5,16,512]{3,2,1,0:T(8,128)(2,1)}, bf16[2,5,16,512]{3,2,1,0:T(8,128)(2,1)S(1)}, u32[]{:S(2)}, u32[]{:S(2)}) collective-permute-start(bf16[2,5,16,512]{3,2,1,0:T(8,128)(2,1)} %get-tuple-element.50), channel_id=1, source_target_pairs={{4,0},{8,4},{12,8},{16,12},{20,16},{24,20},{28,24},{32,28},{36,32}... | collective-permute-start | bytes 491528 | tf_op jit(solution)/shard_map/ppermute | solution.py:539
  115.7 0.0 collective-permute-done.6.rest_1_
  115.7 0.0 collective-permute-done.7.rest_2_
  115.8 0.0 collective-permute-done.8.rest_3_
  115.8 1.6 %shard_map.196 = (bf16[5,64,512]{2,1,0:T(8,128)(2,1)}, bf16[5,64,512]{2,1,0:T(8,128)(2,1)}, bf16[5,64,512]{2,1,0:T(8,128)(2,1)}) custom-call(s32[2]{0:T(128)S(1)} %copy-done.4, bf16[5,16,1536]{2,1,0:T(8,128)(2,1)S(1)} %copy-done.1, bf16[5,16,1536]{2,1,0:T(8,128)(2,1)S(1)} %collective-permute-done.6.rest_1_, ...), custom_call_target="tpu_custom_call" | custom-call | bytes 2000000 | tf_op jit(solution)/shard_map/pallas_call | solution.py:40
  117.4 2.9 %collective-permute-done.5.got_ref = bf16[2,5,16,512]{3,2,1,0:T(8,128)(2,1)S(1)} collective-permute-done((bf16[2,5,16,512]{3,2,1,0:T(8,128)(2,1)}, bf16[2,5,16,512]{3,2,1,0:T(8,128)(2,1)S(1)}, u32[]{:S(2)}, u32[]{:S(2)}) %collective-permute-start.5) | collective-permute-done | bytes 163872 | tf_op jit(solution)/shard_map/ppermute | solution.py:539
  120.2 0.7 copy-done.6
  120.9 1.7 %shard_map.197 = (bf16[5,64,512]{2,1,0:T(8,128)(2,1)}, bf16[5,64,512]{2,1,0:T(8,128)(2,1)}) custom-call(bf16[5,64,512]{2,1,0:T(8,128)(2,1)} %get-tuple-element.47.gk_any, bf16[5,64,512]{2,1,0:T(8,128)(2,1)} %get-tuple-element.48.gv_any, f32[2,5,16,512]{3,2,1,0:T(8,128)} %get-tuple-element.49.tail_ref, ...), custom_call_target="tpu_custom_call", output_to_operand_aliasing={{0}: (0, {}), {1}: (1, {})} | custom-call | bytes 1000000 | tf_op jit(solution)/shard_map/pallas_call | solution.py:553
  122.6 0.0 all-to-all-done.3.in_ref
  122.6 0.7 shard_map.198
  (8 shorter events, 0.0 us)
Async XLA Ops:
  3.0 18.5 %all-to-all-start = ((bf16[4,32,768]{2,1,0:T(8,128)(2,1)}), bf16[4,32,768]{2,1,0:T(8,128)(2,1)S(1)}, u32[]{:S(2)}, u32[]{:S(2)}) async-start(bf16[4,32,768]{2,1,0:T(8,128)(2,1)} %shard_map.189), calls=%async_computation | async-start | bytes 393216 | tf_op jit(solution)/shard_map/all_to_all | solution.py:421
  21.5 30.8 %all-to-all-start.1 = ((bf16[4,5,16,2304]{3,2,1,0:T(8,128)(2,1)}), bf16[4,5,16,2304]{3,2,1,0:T(8,128)(2,1)S(1)}, u32[]{:S(2)}, u32[]{:S(2)}) async-start(bf16[4,5,16,2304]{3,2,1,0:T(8,128)(2,1)} %shard_map.188), calls=%async_computation.1 | async-start | bytes 2949120 | tf_op jit(solution)/shard_map/all_to_all | solution.py:432
  26.3 22.5 %copy-start.3 = (s32[2]{0:T(128)S(1)}, s32[2]{0:T(128)}, u32[]{:S(2)}) copy-start(s32[2]{0:T(128)} %pad_add_fusion.place_ref) | copy-start | bytes 28
  26.3 16.7 %collective-permute-start = (bf16[2,5,16,512]{3,2,1,0:T(8,128)(2,1)S(1)}, bf16[2,5,16,512]{3,2,1,0:T(8,128)(2,1)S(1)}, u32[]{:S(2)}, u32[]{:S(2)}) collective-permute-start(bf16[2,5,16,512]{3,2,1,0:T(8,128)(2,1)S(1)} %pad_maximum_fusion), channel_id=1, source_target_pairs={{0,4},{4,8},{8,12},{12,16},{16,20},{20,24},{24,28},{28,32},{32,36}... | collective-permute-start | bytes 491528 | tf_op jit(solution)/shard_map/ppermute | solution.py:423
  32.4 16.4 %collective-permute-start.1 = (bf16[4,32,768]{2,1,0:T(8,128)(2,1)S(1)}, bf16[4,32,768]{2,1,0:T(8,128)(2,1)S(1)}, u32[]{:S(2)}, u32[]{:S(2)}) collective-permute-start(bf16[4,32,768]{2,1,0:T(8,128)(2,1)S(1)} %all-to-all-done.rest_0_), channel_id=1, source_target_pairs={{0,64},{4,68},{8,72},{12,76},{16,80},{20,84},{24,88},{28,92},{32,9... | collective-permute-start | bytes 589832 | tf_op jit(solution)/shard_map/ppermute | solution.py:448
  35.5 13.2 %collective-permute-start.2 = (bf16[4,32,768]{2,1,0:T(8,128)(2,1)S(1)}, bf16[4,32,768]{2,1,0:T(8,128)(2,1)S(1)}, u32[]{:S(2)}, u32[]{:S(2)}) collective-permute-start(bf16[4,32,768]{2,1,0:T(8,128)(2,1)S(1)} %all-to-all-done.rest_0_), channel_id=1, source_target_pairs={{0,128},{4,132},{8,136},{12,140},{16,144},{20,148},{24,152},{28,15... | collective-permute-start | bytes 589832 | tf_op jit(solution)/shard_map/ppermute | solution.py:448
  39.9 8.9 %collective-permute-start.3 = (bf16[4,32,768]{2,1,0:T(8,128)(2,1)S(1)}, bf16[4,32,768]{2,1,0:T(8,128)(2,1)S(1)}, u32[]{:S(2)}, u32[]{:S(2)}) collective-permute-start(bf16[4,32,768]{2,1,0:T(8,128)(2,1)S(1)} %all-to-all-done.rest_0_), channel_id=1, source_target_pairs={{0,192},{4,196},{8,200},{12,204},{16,208},{20,212},{24,216},{28,22... | collective-permute-start | bytes 589832 | tf_op jit(solution)/shard_map/ppermute | solution.py:448
  43.0 0.7 copy-start.7
  50.4 9.0 %copy-start = (bf16[4,4,32,768]{3,2,1,0:T(8,128)(2,1)}, bf16[4,4,32,768]{3,2,1,0:T(8,128)(2,1)S(1)}, u32[]{:S(2)}) copy-start(bf16[4,4,32,768]{3,2,1,0:T(8,128)(2,1)S(1)} %shard_map.193.mine_ref) | copy-start | bytes 2359300
  50.4 23.2 %collective-permute-start.4 = (bf16[4,4,32,768]{3,2,1,0:T(8,128)(2,1)S(1)}, bf16[4,4,32,768]{3,2,1,0:T(8,128)(2,1)}, u32[]{:S(2)}, u32[]{:S(2)}) collective-permute-start(bf16[4,4,32,768]{3,2,1,0:T(8,128)(2,1)S(1)} %shard_map.193.mine_ref), channel_id=1, source_target_pairs={{0,4},{4,0},{8,12},{12,8},{16,20},{20,16},{24,28},{28,24},{32,36},... | collective-permute-start | bytes 2359304 | tf_op jit(solution)/shard_map/ppermute | solution.py:462
  52.4 1.1 copy-start.5
  59.4 34.9 %all-to-all-start.2 = ((bf16[8,96,1024]{2,1,0:T(8,128)(2,1)}), bf16[8,96,1024]{2,1,0:T(8,128)(2,1)S(1)}, u32[]{:S(2)}, u32[]{:S(2)}) async-start(bf16[8,96,1024]{2,1,0:T(8,128)(2,1)} %bitcast.9), calls=%async_computation.2 | async-start | bytes 3145728 | tf_op jit(solution)/shard_map/all_to_all | solution.py:481
  73.6 20.7 %copy-start.2 = (bf16[128,96]{1,0:T(8,128)(2,1)S(1)}, bf16[128,96]{1,0:T(8,128)(2,1)}, u32[]{:S(2)}) copy-start(bf16[128,96]{1,0:T(8,128)(2,1)} %constant.14.clone.pad_ref) | copy-start | bytes 73732
  80.2 35.5 %collective-permute-start.6 = (bf16[5,16,1536]{2,1,0:T(8,128)(2,1)}, bf16[5,16,1536]{2,1,0:T(8,128)(2,1)S(1)}, u32[]{:S(2)}, u32[]{:S(2)}) collective-permute-start(bf16[5,16,1536]{2,1,0:T(8,128)(2,1)} %get-tuple-element.51), channel_id=1, source_target_pairs={{0,3},{1,0},{2,1},{3,2},{4,7},{5,4},{6,5},{7,6},{8,11},{9,8},{10,9... | collective-permute-start | bytes 737288 | tf_op jit(solution)/shard_map/ppermute | solution.py:409
  85.7 30.0 %collective-permute-start.7 = (bf16[5,16,1536]{2,1,0:T(8,128)(2,1)}, bf16[5,16,1536]{2,1,0:T(8,128)(2,1)S(1)}, u32[]{:S(2)}, u32[]{:S(2)}) collective-permute-start(bf16[5,16,1536]{2,1,0:T(8,128)(2,1)} %get-tuple-element.52), channel_id=1, source_target_pairs={{0,2},{1,3},{2,0},{3,1},{4,6},{5,7},{6,4},{7,5},{8,10},{9,11},{10,... | collective-permute-start | bytes 737288 | tf_op jit(solution)/shard_map/ppermute | solution.py:409
  91.0 24.8 %collective-permute-start.8 = (bf16[5,16,1536]{2,1,0:T(8,128)(2,1)}, bf16[5,16,1536]{2,1,0:T(8,128)(2,1)S(1)}, u32[]{:S(2)}, u32[]{:S(2)}) collective-permute-start(bf16[5,16,1536]{2,1,0:T(8,128)(2,1)} %get-tuple-element.53), channel_id=1, source_target_pairs={{0,1},{1,2},{2,3},{3,0},{4,5},{5,6},{6,7},{7,4},{8,9},{9,10},{10,1... | collective-permute-start | bytes 737288 | tf_op jit(solution)/shard_map/ppermute | solution.py:409
  95.4 27.2 %all-to-all-start.3 = ((bf16[64,16,128]{2,1,0:T(8,128)(2,1)}), bf16[64,16,128]{2,1,0:T(8,128)(2,1)S(1)}, u32[]{:S(2)}, u32[]{:S(2)}) async-start(bf16[64,16,128]{2,1,0:T(8,128)(2,1)} %shard_map.192), calls=%async_computation.3 | async-start | bytes 524288 | tf_op jit(solution)/shard_map/all_to_all | solution.py:563
  105.5 10.3 %copy-start.1 = (bf16[5,16,1536]{2,1,0:T(8,128)(2,1)S(1)}, bf16[5,16,1536]{2,1,0:T(8,128)(2,1)}, u32[]{:S(2)}) copy-start(bf16[5,16,1536]{2,1,0:T(8,128)(2,1)} %get-tuple-element.43.rest_0_) | copy-start | bytes 737284
  105.5 10.3 %copy-start.4 = (s32[2]{0:T(128)S(1)}, s32[2]{0:T(128)}, u32[]{:S(2)}) copy-start(s32[2]{0:T(128)} %pad_add_fusion.place_ref) | copy-start | bytes 28
  112.7 7.6 %collective-permute-start.5 = (bf16[2,5,16,512]{3,2,1,0:T(8,128)(2,1)}, bf16[2,5,16,512]{3,2,1,0:T(8,128)(2,1)S(1)}, u32[]{:S(2)}, u32[]{:S(2)}) collective-permute-start(bf16[2,5,16,512]{3,2,1,0:T(8,128)(2,1)} %get-tuple-element.50), channel_id=1, source_target_pairs={{4,0},{8,4},{12,8},{16,12},{20,16},{24,20},{28,24},{32,28},{36,32}... | collective-permute-start | bytes 491528 | tf_op jit(solution)/shard_map/ppermute | solution.py:539
  120.2 0.7 copy-start.6
